TPU v7x, 1024 devices: a whole 4x8x16 slice. The times are simulated.
1024 devices in a mesh: lat: 32 (over x, y), lon: 32 (over z, core).
Axes of the slice: x: 4, y: 8, z: 16, core: 2. Of those that a mesh axis runs over, the one named last changes fastest.
Arguments:
- right_side: float32 [128, 4096, 512], P('lat', 'lon'), may hold values from -80 to 80
- eofs: bfloat16 [128, 512, 64], P('lat'), may hold values from -0.5 to 0.5
- spectral_gain: float32 [64, 512], P('lon'), may hold values from 0.2 to 2
- diffusivity: float32 [64], replicated, may hold values from 0.05 to 0.25
- flags: int32 [128, 4096], P('lat', 'lon'), may hold values from 0 to 3
- counts: int32 [128, 4096], P('lat', 'lon'), may hold values from 0 to 8
Outputs:
- solution_field: float32 [128, 4096, 512], P('lat', 'lon')
- residual: float32 [128, 4096, 512], P('lat', 'lon')
All inputs are finite; a program needn't handle non-finite values.
Results may differ from a plain program's by a relative error of at most 0.035.
Values may be sent and summed in bfloat16 or wider, within the bound.
A program may use at most 64 MiB of HBM per device.

v0:
```python
import math

import jax
import jax.numpy as jnp
from jax import lax
from jax.sharding import PartitionSpec as P

ITERS = 2


def padded(block, sides, width):
    for axis, dim in sides:
        count = lax.axis_size(axis)
        forward = [(i, i + 1) for i in range(count - 1)]
        backward = [(target, source) for source, target in forward]
        low = lax.ppermute(
            lax.slice_in_dim(block, block.shape[dim] - width, None, axis=dim), axis, forward
        )
        high = lax.ppermute(lax.slice_in_dim(block, 0, width, axis=dim), axis, backward)
        block = jnp.concatenate([low, block, high], axis=dim)
    return block


def weight_of(flags, counts):
    factor = (
        (flags == 0).astype(jnp.float32)
        + 0.5 * (flags == 1).astype(jnp.float32)
        + 0.25 * (flags == 2).astype(jnp.float32)
    )
    return factor * counts.astype(jnp.float32) * 0.25


def spectral_table(rows, nlon, keep):
    points = jnp.arange(rows, dtype=jnp.int32)
    waves = jnp.arange(keep, dtype=jnp.int32)
    phase = points[:, None] * waves[None, :] % nlon
    angle = 2.0 * math.pi / nlon * phase.astype(jnp.float32)
    return jnp.concatenate([jnp.cos(angle), jnp.sin(angle)], axis=1).astype(jnp.bfloat16)


def gain_table(spectral_gain, nlon):
    keep = spectral_gain.shape[1]
    waves = jnp.arange(keep, dtype=jnp.int32)
    factor = jnp.where(waves == 0, 1.0, 2.0).astype(jnp.float32) / nlon
    scaled = spectral_gain * factor[None, :]
    return jnp.concatenate([scaled, scaled], axis=1)


def laplace_step(extended, kappa):
    return extended[1:-1] + kappa * (extended[2:] - 2.0 * extended[1:-1] + extended[:-2])


def local(right_side, eofs, spectral_gain, diffusivity, flags, counts):
    lat_dev, lon_dev, colv = right_side.shape
    nlon = lon_dev * lax.axis_size("lon")
    keep = spectral_gain.shape[1]
    obs_weight = weight_of(flags, counts)[:, :, None]
    full_table = spectral_table(nlon, nlon, keep)
    gain_all = gain_table(spectral_gain, nlon)
    modes_dev = diffusivity.shape[0] // lax.axis_size("lon")
    kappa_local = lax.dynamic_slice_in_dim(
        diffusivity, lax.axis_index("lon") * modes_dev, modes_dev, 0
    )[None, :, None]

    def squares(values):
        return lax.psum(jnp.sum(values * values), ("lat", "lon"))

    solution_field = jnp.zeros_like(right_side)
    residual = right_side
    direction = right_side
    norm_now = squares(residual)
    for step in range(ITERS):
        weighted = (obs_weight * direction).astype(jnp.bfloat16)
        modes = jnp.einsum("lnv,lvm->lmn", weighted, eofs, preferred_element_type=jnp.float32)
        circles = lax.all_to_all(
            modes.astype(jnp.bfloat16), "lon", split_axis=1, concat_axis=2, tiled=True
        ).astype(modes.dtype)
        smooth_values = circles
        for turn in range(2):
            extended = padded(smooth_values.astype(jnp.bfloat16), (("lat", 0),), 1).astype(
                smooth_values.dtype
            )
            smooth_values = laplace_step(extended, kappa_local)
        diffused = smooth_values.astype(jnp.bfloat16)
        coef = jnp.einsum("imn,nk->imk", diffused, full_table, preferred_element_type=jnp.float32)
        scaled = (coef * gain_all[None]).astype(jnp.bfloat16)
        smoothed = jnp.einsum(
            "imk,nk->imn", scaled, full_table, preferred_element_type=jnp.float32
        ).astype(jnp.bfloat16)
        columns = lax.all_to_all(smoothed, "lon", split_axis=2, concat_axis=1, tiled=True)
        expanded = jnp.einsum("lmn,lvm->lnv", columns, eofs, preferred_element_type=jnp.float32)
        image = direction + obs_weight * expanded
        alpha = norm_now / lax.psum(jnp.sum(direction * image), ("lat", "lon"))
        solution_field = solution_field + alpha * direction
        residual = residual - alpha * image
        if step + 1 < ITERS:
            norm_next = squares(residual)
            direction = residual + norm_next / norm_now * direction
            norm_now = norm_next
    return (solution_field, residual)


def solution(mesh):
    in_specs = (
        P("lat", "lon", None),
        P("lat", None, None),
        P("lon", None),
        P(),
        P("lat", "lon"),
        P("lat", "lon"),
    )
    out_specs = (P("lat", "lon", None), P("lat", "lon", None))
    return jax.shard_map(local, mesh=mesh, in_specs=in_specs, out_specs=out_specs, check_vma=False)
```

profile of v0, /device:TPU:1, one launch (start us, length us, event | category | flops | bytes accessed | tf_op | source)
XLA Modules:
  0.0 588.7 jit_solution(13776405568760104823)
XLA Ops:
  0.6 0.0 copy-start
  0.6 0.7 multiply_multiply_fusion
  1.4 0.2 copy-done
  1.6 1.6 fusion.8
  3.2 0.7 copy.16
  3.9 20.4 %all-to-all-start = ((bf16[4,64,128]{2,0,1:T(4,128)(2,1)}), bf16[4,64,128]{2,0,1:T(4,128)(2,1)S(1)}, u32[]{:S(2)}, u32[]{:S(2)}) async-start(bf16[4,64,128]{2,0,1:T(4,128)(2,1)} %copy.16), calls=%async_computation | async-start | bytes 131072 | tf_op jit(solution)/shard_map/all_to_all | solution.py:75
  24.3 0.0 copy-start.2
  24.3 0.0 copy-start.3
  24.3 34.9 %sine_convert_fusion = (bf16[4096,512]{1,0:T(8,128)(2,1)}, bf16[4096,512]{1,0:T(8,128)(2,1)}) fusion(), kind=kLoop, calls=%fused_computation.7 | loop fusion | flops 33554432 | bytes 8388608 | tf_op jit(solution)/shard_map/convert.1
  59.2 0.0 all-to-all-done
  59.3 1.3 collective-permute-start.1
  60.6 4.0 collective-permute-start
  64.6 0.0 copy-done.2
  64.6 0.0 copy-done.3
  64.6 0.1 dynamic_slice.3
  64.7 0.0 collective-permute-done.1
  64.7 0.7 collective-permute-done
  65.5 0.1 maximum_convert_fusion
  65.6 0.1 fusion.22
  65.7 3.6 collective-permute-start.2
  69.4 1.3 collective-permute-start.3
  70.7 0.0 collective-permute-done.2
  70.7 3.2 collective-permute-done.3
  73.9 0.1 maximum_convert_fusion.1
  74.0 0.1 fusion.23
  74.1 9.3 %convolution_convert_fusion.1 = bf16[4,2,4096]{2,0,1:T(4,128)(2,1)S(1)} fusion(bf16[4096,512]{1,0:T(8,128)(2,1)} %get-tuple-element.19, bf16[4096,512]{1,0:T(8,128)(2,1)} %get-tuple-element.20, bf16[4,2,4096]{2,1,0:T(2,128)(2,1)S(1)} %fusion.23, f32[2,1024]{1,0:T(2,128)S(1)} %pad_maximum_fusion), kind=kOutput, calls=%fused_computation.13 | convolution fusion | flops 167821312 | bytes 8527872 | tf_op jit(solution)/shard_map/imk,nk->imn/dot_general | solution.py:87
  83.5 0.0 copy-start.1
  83.5 2.9 copy.19
  86.4 4.0 reshape.18
  90.4 27.9 %all_to_all.72 = bf16[32,2,512]{2,1,0:T(2,128)(2,1)S(1)} all-to-all(bf16[32,2,512]{2,1,0:T(2,128)(2,1)S(1)} %reshape.18), channel_id=1, replica_groups=mesh['lat'=32,'lon'=32] {'lon'}, dimensions={0} | all-to-all | bytes 131072 | tf_op jit(solution)/shard_map/all_to_all | solution.py:90
  118.3 4.5 reshape.19
  122.8 2.2 copy.20
  125.0 0.0 copy-done.1
  125.0 1.1 multiply_reduce_fusion.2
  126.1 126.1 %all-reduce = (f32[]{:T(128)}, f32[]{:T(128)}) all-reduce(f32[]{:T(128)} %get-tuple-element.3, f32[]{:T(128)} %get-tuple-element.2), channel_id=1, replica_groups=mesh['lat'=32,'lon'=32] {'lat','lon'}, use_global_device_ids=true, to_apply=%region_1.2 | all-reduce | flops 2 | bytes 16 | tf_op jit(solution)/shard_map/psum | solution.py:66
  253.6 0.9 multiply_reduce_fusion.1
  254.5 118.3 %psum.30 = f32[]{:T(128)} all-reduce(f32[]{:T(128)} %multiply_reduce_fusion.1), channel_id=1, replica_groups=mesh['lat'=32,'lon'=32] {'lat','lon'}, use_global_device_ids=true, to_apply=%region_5.6 | all-reduce | flops 1 | bytes 8 | tf_op jit(solution)/shard_map/psum | solution.py:66
  374.2 0.2 multiply_add_fusion.1
  374.4 0.4 fusion.9
  374.8 0.1 copy.21
  374.8 19.6 %all_to_all.73 = bf16[4,64,128]{2,0,1:T(4,128)(2,1)S(1)} all-to-all(bf16[4,64,128]{2,0,1:T(4,128)(2,1)S(1)} %copy.21), channel_id=1, replica_groups=mesh['lat'=32,'lon'=32] {'lon'}, dimensions={1} | all-to-all | bytes 131072 | tf_op jit(solution)/shard_map/all_to_all | solution.py:75
  394.4 0.6 slice.89
  395.1 0.6 slice.91
  395.7 1.3 collective-permute-start.5
  397.0 4.6 collective-permute-start.4
  401.6 0.0 collective-permute-done.5
  401.6 0.4 collective-permute-done.4
  402.0 0.9 maximum_convert_fusion.2
  402.9 0.1 fusion.24
  403.1 3.7 collective-permute-start.6
  406.8 1.3 collective-permute-start.7
  408.1 0.0 collective-permute-done.6
  408.1 3.2 collective-permute-done.7
  411.3 0.1 maximum_convert_fusion.3
  411.4 0.1 fusion.25
  411.5 9.3 %convolution_convert_fusion = bf16[4,2,4096]{2,0,1:T(4,128)(2,1)S(1)} fusion(bf16[4096,512]{1,0:T(8,128)(2,1)} %get-tuple-element.19, bf16[4096,512]{1,0:T(8,128)(2,1)} %get-tuple-element.20, bf16[4,2,4096]{2,1,0:T(2,128)(2,1)S(1)} %fusion.25, f32[2,1024]{1,0:T(2,128)S(1)} %pad_maximum_fusion), kind=kOutput, calls=%fused_computation.12 | convolution fusion | flops 167821312 | bytes 8527872 | tf_op jit(solution)/shard_map/imk,nk->imn/dot_general | solution.py:87
  420.9 3.9 copy.24
  424.8 4.9 reshape.20
  429.8 20.1 %all_to_all.74 = bf16[32,2,512]{2,1,0:T(2,128)(2,1)S(1)} all-to-all(bf16[32,2,512]{2,1,0:T(2,128)(2,1)S(1)} %reshape.20), channel_id=1, replica_groups=mesh['lat'=32,'lon'=32] {'lon'}, dimensions={0} | all-to-all | bytes 131072 | tf_op jit(solution)/shard_map/all_to_all | solution.py:90
  449.9 5.5 reshape.21
  455.4 4.8 copy.25
  460.2 2.0 multiply_reduce_fusion
  462.2 122.0 %psum.31 = f32[]{:T(128)} all-reduce(f32[]{:T(128)} %get-tuple-element.17), channel_id=1, replica_groups=mesh['lat'=32,'lon'=32] {'lat','lon'}, use_global_device_ids=true, to_apply=%region_7.8 | all-reduce | flops 1 | bytes 8 | tf_op jit(solution)/shard_map/psum | solution.py:93
  585.6 3.1 multiply_subtract_fusion
  (13 shorter events, 0.2 us)
Async XLA Ops:
  0.6 1.0 copy-start
  3.9 55.3 %all-to-all-start = ((bf16[4,64,128]{2,0,1:T(4,128)(2,1)}), bf16[4,64,128]{2,0,1:T(4,128)(2,1)S(1)}, u32[]{:S(2)}, u32[]{:S(2)}) async-start(bf16[4,64,128]{2,0,1:T(4,128)(2,1)} %copy.16), calls=%async_computation | async-start | bytes 131072 | tf_op jit(solution)/shard_map/all_to_all | solution.py:75
  24.3 40.3 %copy-start.2 = (f32[2,512]{1,0:T(2,128)S(1)}, f32[2,512]{1,0:T(2,128)}, u32[]{:S(2)}) copy-start(f32[2,512]{1,0:T(2,128)} %param.8) | copy-start | bytes 12292
  24.3 40.3 %copy-start.3 = (f32[64]{0:T(128)S(1)}, f32[64]{0:T(128)}, u32[]{:S(2)}) copy-start(f32[64]{0:T(128)} %param.9) | copy-start | bytes 772
  59.3 5.4 collective-permute-start.1
  60.6 4.8 collective-permute-start
  65.7 4.9 collective-permute-start.2
  69.4 4.5 collective-permute-start.3
  83.5 41.5 %copy-start.1 = (f32[4,128,512]{2,1,0:T(8,128)S(1)}, f32[4,128,512]{2,1,0:T(8,128)}, u32[]{:S(2)}) copy-start(f32[4,128,512]{2,1,0:T(8,128)} %param.6) | copy-start | bytes 3145732
  395.7 5.9 %collective-permute-start.5 = (bf16[1,2,4096]{2,1,0:T(2,128)(2,1)}, bf16[1,2,4096]{2,1,0:T(2,128)(2,1)}, u32[]{:S(2)}, u32[]{:S(2)}) collective-permute-start(bf16[1,2,4096]{2,1,0:T(2,128)(2,1)} %slice.91), channel_id=1, source_target_pairs={{32,0},{64,32},{96,64},{128,96},{160,128},{192,160},{224,192},{256... | collective-permute-start | bytes 49160 | tf_op jit(solution)/shard_map/ppermute | solution.py:19
  397.0 5.1 collective-permute-start.4
  403.1 5.0 collective-permute-start.6
  406.8 4.5 collective-permute-start.7
where the time goes:
time: 590 us; the launch traced here: 589 us
  blocking collectives  434 us (74%)
  other arithmetic  41.6 us (7%)
  starting transfers between devices  41.5 us (7%)
  local copies, waits for them, and re-layouts  35.2 us (6%)
  matrix products  23.7 us (4%)
  waiting for transfers between devices  7.49 us (1%)
    psum x2, blocking collectives, squares(): return lax.psum(jnp.sum(values * values), ('lat', 'lon'))  244 us
    psum x1, blocking collectives, local(): alpha = norm_now / lax.psum(jnp.sum(direction * image), ('lat', 'lon'))  122 us
    all_to_all x2, blocking collectives, local(): lax.all_to_all(smoothed, 'lon', split_axis=2, concat_axis=1, tiled=True)  48 us
    another operation x1, other arithmetic  34.9 us
    all_to_all x1, starting transfers between devices, local(): lax.all_to_all(modes.astype(jnp.bfloat16), 'lon', split_axis=1, concat_ax...  20.4 us
    all_to_all x1, blocking collectives, local(): lax.all_to_all(modes.astype(jnp.bfloat16), 'lon', split_axis=1, concat_ax...  19.6 us
    unnamed x12, local copies, waits for them, and re-layouts  19.2 us
    dot_general x2, matrix products, local(): jnp.einsum('imk,nk->imn', scaled, full_table, preferred_element_type=jnp....  18.7 us
  transfers between devices with their start and end apart: 9, of which 4 were waited for; matrix products, arithmetic and copies ran while one was open for 6% of the time, Pallas kernels for 0%

commit v1 on v0

v1 whole, which is shorter than its diff:
```python
import math

import jax
import jax.numpy as jnp
import numpy as np
from jax import lax
from jax.experimental import pallas as pl
from jax.experimental.pallas import tpu as pltpu
from jax.sharding import PartitionSpec as P

MESH = pl.DeviceIdType.MESH
F32, BF16 = jnp.float32, jnp.bfloat16
ROWS, MODES, COLV, NLON, KEEP = 4, 64, 512, 4096, 512
LON, ZS, PTS = 32, 16, 128
K1 = 9
SPEC = K1 * MODES
GROUP = 16
OWNER_STEP = LON // ROWS

C1, C3, RT = math.cos(math.pi / 8), math.sin(math.pi / 8), math.sqrt(0.5)


def tables():
    kk = np.arange(32)
    signed = np.concatenate([kk, -1 - kk])
    j = np.arange(256)
    angle = 2.0 * np.pi * ((j[:, None] * signed[None, :]) % 256) / 256.0
    cos, sin = np.cos(angle), np.sin(angle)
    re_in = np.concatenate([cos[:, :32], sin[:, :32], cos[:, 32:], sin[:, 32:]], axis=1)
    im_in = np.concatenate([-sin[:, :32], cos[:, :32], -sin[:, 32:], cos[:, 32:]], axis=1)
    wave = np.stack([re_in.reshape(2, PTS, 128), im_in.reshape(2, PTS, 128)], axis=1)
    wave = wave.reshape(2, 2 * PTS, 128)
    k1 = np.arange(K1)
    phase = 2.0 * np.pi * ((k1[:, None] * j[None, :]) % NLON) / NLON
    twist = np.stack([np.cos(phase), np.sin(phase)], axis=1)
    twist = twist.reshape(2 * K1, 2, PTS).transpose(1, 0, 2)
    pick = np.zeros((KEEP, K1, 128))
    for one in range(K1):
        for lane in range(128):
            part, at = lane // 32, lane % 32
            if part < 2:
                k = one + 16 * at
            elif 1 <= one <= 7:
                k = 16 * at + 16 - one
            else:
                continue
            pick[k, one, lane] = (1.0 if k == 0 else 2.0) / NLON
    pick = pick.reshape(KEEP, K1 * 128)
    return (
        jnp.asarray(wave.astype(jnp.bfloat16)),
        jnp.asarray(twist.astype(np.float32)),
        jnp.asarray(pick.astype(jnp.bfloat16)),
    )


def cosines(p):
    e = [p[0] + p[8], p[1] + p[7], p[2] + p[6], p[3] + p[5], p[4]]
    o = [p[0] - p[8], p[1] - p[7], p[2] - p[6], p[3] - p[5]]
    f0, f1 = e[0] + e[4], e[1] + e[3]
    f02 = f0 + e[2]
    g0, g1 = e[0] - e[4], RT * (e[1] - e[3])
    o2 = RT * o[2]
    a, b = o[0] + o2, o[0] - o2
    u, v = C1 * o[1] + C3 * o[3], C3 * o[1] - C1 * o[3]
    return [f02 + f1, a + u, g0 + g1, b + v, f0 - e[2], b - v, g0 - g1, a - u, f02 - f1]


def sines(q):
    h = [None, q[1] + q[7], q[2] + q[6], q[3] + q[5], q[4]]
    d = [None, q[1] - q[7], q[2] - q[6], q[3] - q[5]]
    r = RT * (d[1] + d[3])
    h2 = RT * h[2]
    m, n = h2 + h[4], h2 - h[4]
    u, v = C3 * h[1] + C1 * h[3], C1 * h[1] - C3 * h[3]
    return [None, u + m, r + d[2], v + n, d[1] - d[3], v - n, r - d[2], u - m]


def column_of(row, size):
    at = lax.broadcasted_iota(jnp.int32, (size, size), 0)
    to = lax.broadcasted_iota(jnp.int32, (size, size), 1)
    spread = jnp.where(at == to, jnp.broadcast_to(row, (size, size)), 0.0)
    return jnp.sum(spread, axis=1, keepdims=True)


def by_lane(values):
    part = values[:, 0:128] + values[:, 128:256] + values[:, 256:384] + values[:, 384:512]
    return jnp.sum(part, axis=0, keepdims=True)


def kernel(
    lats,
    b_hbm, e_hbm, gain_ref, kappa_ref, flags_ref, counts_ref, wave_hbm, twist_hbm, pick_hbm,
    x_hbm, r_hbm,
    b, e, wave, twist, pick, y0, halo_out, halo_in, halo_in2,
    aux_g, aux_w, got_g, got_w, to_owner, rows_in, zbuf, bbuf, gains, y1,
    s_out, f_out, s_in, f_in, tbuf, ubuf, part, ar1, mid, ar2, xo, ro,
    ld, aux_s, aux_r, halo_s, halo_r, own_s, own_r, ret_s, ret_r, ar_s, ar_r, out_s,
):
    lat, me = lax.axis_index("lat"), lax.axis_index("lon")
    owner = lax.rem(me, OWNER_STEP) == 0
    my_row = lax.div(me, OWNER_STEP)

    barrier = pltpu.get_barrier_semaphore()

    def greet_lon(o, carry):
        pl.semaphore_signal(
            barrier, inc=1, device_id=(lat, lax.rem(me + o, LON)), device_id_type=MESH
        )
        return carry

    def greet_lat(o, carry):
        pl.semaphore_signal(
            barrier, inc=1, device_id=(lax.rem(lat + o, lats), me), device_id_type=MESH
        )
        return carry

    loads = [
        pltpu.make_async_copy(b_hbm, b, ld.at[0]),
        pltpu.make_async_copy(e_hbm, e, ld.at[1]),
    ]
    for load in loads:
        load.start()
    lax.fori_loop(1, LON, greet_lon, 0)
    lax.fori_loop(1, lats, greet_lat, 0)

    owner_loads = [
        pltpu.make_async_copy(wave_hbm, wave, ld.at[2]),
        pltpu.make_async_copy(twist_hbm, twist, ld.at[3]),
        pltpu.make_async_copy(pick_hbm, pick, ld.at[4]),
    ]

    @pl.when(owner)
    def _():
        for load in owner_loads:
            load.start()

    flags = flags_ref[...]
    factor = (
        (flags == 0).astype(F32) + 0.5 * (flags == 1).astype(F32) + 0.25 * (flags == 2).astype(F32)
    )
    weight = factor * counts_ref[...].astype(F32) * 0.25
    w_col = [column_of(weight[r : r + 1, :], PTS) for r in range(ROWS)]
    kappa = column_of(kappa_ref[...], MODES)
    for mode in range(2):
        for quarter in range(4):
            at = mode * 4 + quarter
            aux_g[at : at + 1, :] = gain_ref[mode : mode + 1, quarter * 128 : quarter * 128 + 128]
    for r in range(ROWS):
        aux_w[r] = jnp.broadcast_to(weight[r : r + 1, :], (8, PTS))

    for load in loads:
        load.wait()
    for r in range(ROWS):
        weighted = (w_col[r] * b[r]).astype(BF16)
        modes = jnp.dot(weighted, e[r], preferred_element_type=F32).T
        y0[r] = modes
        halo_out[r] = modes.astype(BF16)

    pl.semaphore_wait(barrier, LON - 1 + lats - 1)

    down, up = lax.rem(lat + lats - 1, lats), lax.rem(lat + 1, lats)

    def halo(source, target, at):
        copies = [
            pltpu.make_async_remote_copy(
                source.at[pl.ds(2 * way, 2)], target.at[1 - way],
                halo_s.at[at + way], halo_r.at[at + way],
                device_id=(peer, me), device_id_type=MESH,
            )
            for way, peer in ((0, down), (1, up))
        ]
        for copy in copies:
            copy.start()
        return copies

    def diffuse(rows, halos):
        low, high = lat > 0, lat < lats - 1
        ext = [jnp.where(low, halos[0, i].astype(F32), 0.0) for i in range(2)]
        ext += rows
        ext += [jnp.where(high, halos[1, i].astype(F32), 0.0) for i in range(2)]
        once = [
            ext[i] + kappa * (ext[i + 1] - 2.0 * ext[i] + ext[i - 1]) for i in range(1, 7)
        ]
        once[0] = jnp.where(low, once[0], 0.0)
        once[5] = jnp.where(high, once[5], 0.0)
        return [
            once[i] + kappa * (once[i + 1] - 2.0 * once[i] + once[i - 1]) for i in range(1, 5)
        ]

    first_halo = halo(halo_out, halo_in, 0)

    for r in range(ROWS):
        at = r * OWNER_STEP

        @pl.when(me != at)
        def _():
            for source, target, which in ((aux_g, got_g, 0), (aux_w.at[r], got_w, 1)):
                pltpu.make_async_remote_copy(
                    source, target.at[pl.ds(pl.multiple_of(8 * me, 8), 8)],
                    aux_s.at[which], aux_r.at[which],
                    device_id=(lat, at), device_id_type=MESH,
                ).start()

        @pl.when(me == at)
        def _():
            got_g[pl.ds(pl.multiple_of(8 * me, 8), 8), :] = aux_g[...]
            got_w[pl.ds(pl.multiple_of(8 * me, 8), 8), :] = aux_w[r]

    for copy in first_halo:
        copy.wait()
    diffused = diffuse([y0[r] for r in range(ROWS)], halo_in)
    for r in range(ROWS):
        to_owner[r] = diffused[r].astype(BF16)
    for r in range(ROWS):
        at = r * OWNER_STEP

        @pl.when(me != at)
        def _():
            pltpu.make_async_remote_copy(
                to_owner.at[r], rows_in.at[me], own_s.at[0], own_r.at[0],
                device_id=(lat, at), device_id_type=MESH,
            ).start()

        @pl.when(me == at)
        def _():
            rows_in[me] = to_owner[r]

    def settle(buffer, count, semaphore):
        view = buffer.at[pl.ds(0, count)]
        pltpu.make_async_copy(view, view, semaphore).wait()

    def smooth(source, target):
        def forward(g, carry):
            c, rows = lax.div(g, 4), pl.ds(pl.multiple_of(lax.rem(g, 4) * GROUP, GROUP), GROUP)
            x = [source[2 * z + c, rows, :].astype(F32) for z in range(ZS)]
            p = [x[0]] + [x[z] + x[16 - z] for z in range(1, 8)] + [x[8]]
            q = [None] + [x[z] - x[16 - z] for z in range(1, 8)]
            real, imag = cosines(p), sines(q)
            for k1 in range(K1):
                to = pl.ds(pl.multiple_of(k1 * MODES + lax.rem(g, 4) * GROUP, GROUP), GROUP)
                if k1 == 0:
                    re, im = real[0], jnp.zeros_like(real[0])
                else:
                    cos = twist[c, pl.ds(2 * k1, 1), :]
                    sin = twist[c, pl.ds(2 * k1 + 1, 1), :]
                    if k1 == 8:
                        re, im = real[8] * cos, real[8] * sin
                    else:
                        re = real[k1] * cos - imag[k1] * sin
                        im = real[k1] * sin + imag[k1] * cos
                zbuf[c, to, 0:PTS] = re.astype(BF16)
                zbuf[c, to, PTS : 2 * PTS] = im.astype(BF16)
            return carry

        lax.fori_loop(0, 8, forward, 0)
        for chunk in range(3):
            rows = pl.ds(chunk * 192, 192)
            coef = jnp.dot(zbuf[0, rows, :], wave[0], preferred_element_type=F32)
            coef = coef + jnp.dot(zbuf[1, rows, :], wave[1], preferred_element_type=F32)
            scaled = (coef * gains[rows, :]).astype(BF16)
            for c in range(2):
                bbuf[c, rows, :] = lax.dot_general(
                    scaled, wave[c], (((1,), (1,)), ((), ())), preferred_element_type=F32
                )

        def inverse(g, carry):
            c, rows = lax.div(g, 4), pl.ds(pl.multiple_of(lax.rem(g, 4) * GROUP, GROUP), GROUP)
            real, imag = [], [None]
            for k1 in range(K1):
                at = pl.ds(pl.multiple_of(k1 * MODES + lax.rem(g, 4) * GROUP, GROUP), GROUP)
                re = bbuf[c, at, 0:PTS]
                if k1 == 0:
                    real.append(re)
                    continue
                im = bbuf[c, at, PTS : 2 * PTS]
                cos = twist[c, pl.ds(2 * k1, 1), :]
                sin = twist[c, pl.ds(2 * k1 + 1, 1), :]
                real.append(re * cos + im * sin)
                if k1 < 8:
                    imag.append(im * cos - re * sin)
            even, odd = cosines(real), sines(imag)
            target[c, rows, :] = even[0].astype(BF16)
            target[16 + c, rows, :] = even[8].astype(BF16)
            for z in range(1, 8):
                target[2 * z + c, rows, :] = (even[z] + odd[z]).astype(BF16)
                target[2 * (16 - z) + c, rows, :] = (even[z] - odd[z]).astype(BF16)
            return carry

        lax.fori_loop(0, 8, inverse, 0)

    def give_back(source, target, which):
        def send(o):
            peer = lax.rem(me + o, LON)
            pltpu.make_async_remote_copy(
                source.at[peer], target.at[my_row], ret_s.at[which], ret_r.at[which],
                device_id=(lat, peer), device_id_type=MESH,
            ).start()

        def pair(o, carry):
            send(16 - o)
            send(16 + o)
            return carry

        send(16)
        lax.fori_loop(1, 16, pair, 0)
        target[my_row] = source[me]

    @pl.when(owner)
    def _():
        for load in owner_loads:
            load.wait()
        transposed = e[my_row].astype(F32).T.astype(BF16)
        gram = jnp.dot(transposed, e[my_row], preferred_element_type=F32)
        gram_high = gram.astype(BF16)
        gram_low = (gram - gram_high.astype(F32)).astype(BF16)
        gram_both = jnp.concatenate([gram_high.astype(F32), gram_low.astype(F32)], axis=1).astype(BF16)

        settle(got_g.reshape(LON, 8, 128), LON - 1, aux_r.at[0])
        settle(got_w.reshape(LON, 8, 128), LON - 1, aux_r.at[1])
        spread = jnp.concatenate([got_g[pl.ds(q, MODES, stride=4), :] for q in range(4)], axis=1)
        first = spread.astype(BF16)
        rest = spread - first.astype(F32)
        second = rest.astype(BF16)
        third = (rest - second.astype(F32)).astype(BF16)
        for k1 in range(K1):
            lanes = pl.ds(k1 * 128, 128)
            total = jnp.dot(first, pick[:, lanes], preferred_element_type=F32)
            total = total + jnp.dot(second, pick[:, lanes], preferred_element_type=F32)
            total = total + jnp.dot(third, pick[:, lanes], preferred_element_type=F32)
            gains[pl.ds(k1 * MODES, MODES), :] = total

        settle(rows_in, LON - 1, own_r.at[0])
        smooth(rows_in, s_out)
        give_back(s_out, s_in, 0)

        for z in range(ZS):
            pair = jnp.concatenate([s_out[2 * z], s_out[2 * z + 1]], axis=1)
            product = jnp.dot(
                gram_both, jnp.concatenate([pair, pair], axis=0), preferred_element_type=F32
            )
            for c in range(2):
                row = got_w[pl.ds(8 * (2 * z + c), 1), :]
                y1[2 * z + c] = product[:, c * PTS : c * PTS + PTS] * (row * row)
        smooth(y1, f_out)
        give_back(f_out, f_in, 1)

    def expand(values, r):
        return w_col[r] * lax.dot_general(
            values.T.astype(BF16), e[r], (((1,), (1,)), ((), ())), preferred_element_type=F32
        )

    def arrived(buffer, which):
        @pl.when(owner)
        def _():
            settle(buffer, ROWS - 1, ret_r.at[which])

        @pl.when(jnp.logical_not(owner))
        def _():
            settle(buffer, ROWS, ret_r.at[which])

    arrived(s_in, 0)
    sums = [jnp.zeros((1, PTS), F32) for _ in range(4)]
    for r in range(ROWS):
        t = expand(s_in[r].astype(F32), r)
        tbuf[r] = t
        values = b[r]
        sums[0] = sums[0] + by_lane(values * values)
        sums[1] = sums[1] + by_lane(values * t)
        sums[2] = sums[2] + by_lane(t * t)

    arrived(f_in, 1)
    second_halo = halo(f_in, halo_in2, 2)
    for copy in second_halo:
        copy.wait()
    diffused = diffuse([f_in[r].astype(F32) for r in range(ROWS)], halo_in2)
    for r in range(ROWS):
        u = expand(diffused[r], r)
        ubuf[r] = u
        sums[3] = sums[3] + by_lane(tbuf[r] * u)
    part[...] = jnp.concatenate(sums + [jnp.zeros((4, PTS), F32)], axis=0)

    def share(source, target, mine, count, which, device):
        def send(o, carry):
            pltpu.make_async_remote_copy(
                source, target.at[mine], ar_s.at[which], ar_r.at[which],
                device_id=device(o), device_id_type=MESH,
            ).start()
            return carry

        lax.fori_loop(1, count, send, 0)
        target[mine] = source[...]
        settle(target, count - 1, ar_r.at[which])
        total = target[0]
        for i in range(1, count):
            total = total + target[i]
        return total

    mid[...] = share(part, ar1, me, LON, 0, lambda o: (lat, lax.rem(me + o, LON)))
    total = share(mid, ar2, lat, lats, 1, lambda o: (lax.rem(lat + o, lats), me))
    total = jnp.sum(total, axis=1, keepdims=True)
    norm = total[0:1]
    m1, m2, m3 = total[1:2] / norm, total[2:3] / norm, total[3:4] / norm
    alpha = 1.0 / (1.0 + m1)
    spread2 = m2 - m1 * m1
    spread3 = m3 - 3.0 * m1 * m2 + 2.0 * m1 * m1 * m1
    beta = alpha * alpha * spread2
    alpha_next = alpha * spread2 / (spread2 * (1.0 - beta) + alpha * spread3)
    along = alpha * m1 + beta
    x_b, x_t = alpha + alpha_next * along, -alpha_next * alpha
    r_b = alpha * m1 - alpha_next * along
    r_t = -(alpha + alpha_next * (along - alpha))
    r_u = alpha_next * alpha

    writes = []
    for r in range(ROWS):
        xo[r] = x_b * b[r] + x_t * tbuf[r]
        ro[r] = r_b * b[r] + r_t * tbuf[r] + r_u * ubuf[r]
        for source, target, at in ((xo, x_hbm, 0), (ro, r_hbm, 1)):
            write = pltpu.make_async_copy(source.at[r], target.at[r], out_s.at[at, r])
            write.start()
            writes.append(write)
    for write in writes:
        write.wait()

    @pl.when(owner)
    def _():
        settle(aux_w, ROWS - 1, aux_s.at[0])
        settle(aux_w, ROWS - 1, aux_s.at[1])
        settle(to_owner, ROWS - 1, own_s.at[0])
        settle(s_out, LON - 1, ret_s.at[0])
        settle(f_out, LON - 1, ret_s.at[1])

    @pl.when(jnp.logical_not(owner))
    def _():
        settle(aux_w, ROWS, aux_s.at[0])
        settle(aux_w, ROWS, aux_s.at[1])
        settle(to_owner, ROWS, own_s.at[0])

    settle(ar1, LON - 1, ar_s.at[0])
    settle(ar2, lats - 1, ar_s.at[1])


def local(right_side, eofs, spectral_gain, diffusivity, flags, counts):
    lats = lax.axis_size("lat")
    wave, twist, pick = tables()
    anywhere = pl.BlockSpec(memory_space=pl.ANY)
    vmem = pl.BlockSpec(memory_space=pltpu.VMEM)
    like = jax.ShapeDtypeStruct(right_side.shape, F32)
    dma, vm = pltpu.SemaphoreType.DMA, pltpu.VMEM

    def whole(*args):
        kernel(lats, *args)

    return pl.pallas_call(
        whole,
        out_shape=(like, like),
        in_specs=[anywhere, anywhere, vmem, vmem, vmem, vmem, anywhere, anywhere, anywhere],
        out_specs=(anywhere, anywhere),
        scratch_shapes=[
            vm((ROWS, PTS, COLV), F32),
            vm((ROWS, COLV, MODES), BF16),
            vm((2, 2 * PTS, 128), BF16),
            vm((2, 2 * K1, PTS), F32),
            vm((KEEP, K1 * 128), BF16),
            vm((ROWS, MODES, PTS), F32),
            vm((ROWS, MODES, PTS), BF16),
            vm((2, 2, MODES, PTS), BF16),
            vm((2, 2, MODES, PTS), BF16),
            vm((8, 128), F32),
            vm((ROWS, 8, PTS), F32),
            vm((LON * 8, 128), F32),
            vm((LON * 8, PTS), F32),
            vm((ROWS, MODES, PTS), BF16),
            vm((LON, MODES, PTS), BF16),
            vm((2, SPEC, 2 * PTS), BF16),
            vm((2, SPEC, 2 * PTS), F32),
            vm((SPEC, 128), F32),
            vm((LON, MODES, PTS), F32),
            vm((LON, MODES, PTS), BF16),
            vm((LON, MODES, PTS), BF16),
            vm((ROWS, MODES, PTS), BF16),
            vm((ROWS, MODES, PTS), BF16),
            vm((ROWS, PTS, COLV), F32),
            vm((ROWS, PTS, COLV), F32),
            vm((8, PTS), F32),
            vm((LON, 8, PTS), F32),
            vm((8, PTS), F32),
            vm((lats, 8, PTS), F32),
            vm((ROWS, PTS, COLV), F32),
            vm((ROWS, PTS, COLV), F32),
            dma((5,)),
            dma((2,)),
            dma((2,)),
            dma((4,)),
            dma((4,)),
            dma((1,)),
            dma((1,)),
            dma((2,)),
            dma((2,)),
            dma((2,)),
            dma((2,)),
            dma((2, ROWS)),
        ],
        compiler_params=pltpu.CompilerParams(
            collective_id=0, has_side_effects=True, vmem_limit_bytes=40 * 2**20
        ),
    )(
        right_side, eofs, spectral_gain, diffusivity.reshape(1, MODES), flags, counts,
        wave, twist, pick,
    )


def solution(mesh):
    in_specs = (
        P("lat", "lon", None),
        P("lat", None, None),
        P("lon", None),
        P(),
        P("lat", "lon"),
        P("lat", "lon"),
    )
    out_specs = (P("lat", "lon", None), P("lat", "lon", None))
    return jax.shard_map(local, mesh=mesh, in_specs=in_specs, out_specs=out_specs, check_vma=False)
```

time: 590 us -> 80.4 us (0.14)
  blocking collectives: 434 us -> 0 us
  Pallas kernels: 0 us -> 69.3 us
  other arithmetic: 41.6 us -> 0 us
  starting transfers between devices: 41.5 us -> 0 us
  local copies, waits for them, and re-layouts: 35.2 us -> 10 us
  matrix products: 23.7 us -> 0 us
  waiting for transfers between devices: 7.49 us -> 0 us
    psum x3 -> x0, blocking collectives: 366 us -> none  [the longest x2 244 us: squares(): return lax.psum(jnp.sum(values * values), ('lat', 'lon'))]
    pallas_call x0 -> x1, Pallas kernels: none -> 69.3 us  [local(): pl.pallas_call(whole, out_shape=(like, like), in_specs=[anywhere, anywher...]
    all_to_all x3 -> x0, blocking collectives: 67.6 us -> none  [the longest x2 48 us: local(): lax.all_to_all(smoothed, 'lon', split_axis=2, concat_axis=1, tiled=True)]
    another operation x1 -> x0, other arithmetic: 34.9 us -> none
    dot_general x6 -> x0, matrix products: 23.7 us -> none  [the longest x2 18.7 us: local(): jnp.einsum('imk,nk->imn', scaled, full_table, preferred_element_type=jnp....]
    ppermute x8 -> x0, starting transfers between devices: 21.1 us -> none  [the longest x4 15.9 us: padded(): lax.ppermute(lax.slice_in_dim(block, block.shape[dim] - width, None, axis...]
    all_to_all x1 -> x0, starting transfers between devices: 20.4 us -> none  [local(): lax.all_to_all(modes.astype(jnp.bfloat16), 'lon', split_axis=1, concat_ax...]
    unnamed x12 -> x19, local copies, waits for them, and re-layouts: 19.2 us -> 10 us
  transfers between devices with their start and end apart: 9 -> 0, of which waited for: 4 -> 0; matrix products, arithmetic and copies ran while one was open for 6% -> 0% of each run, Pallas kernels for 0% -> 0%
where the time goes in v1:
time: 80.4 us; the launch traced here: 80 us
  Pallas kernels  69.3 us (86%)
  local copies, waits for them, and re-layouts  10 us (12%)
    pallas_call x1, Pallas kernels, local(): pl.pallas_call(whole, out_shape=(like, like), in_specs=[anywhere, anywher...  69.3 us
    unnamed x19, local copies, waits for them, and re-layouts  10 us

profile of v1, /device:TPU:1, one launch (start us, length us, event | category | flops | bytes accessed | tf_op | source)
XLA Modules:
  0.0 80.0 jit_solution(17194044095245751349)
XLA Ops:
  0.6 1.2 %copy.11.args_1_ = bf16[4,512,64]{2,1,0:T(8,128)(2,1)S(1)} copy(bf16[4,512,64]{1,2,0:T(8,128)(2,1)} %param.10) | data formatting | bytes 524288 | tf_op args[1]
  1.9 0.0 copy-start
  1.9 1.3 %copy-done = bf16[512,1152]{1,0:T(8,128)(2,1)S(1)} copy-done((bf16[512,1152]{1,0:T(8,128)(2,1)S(1)}, bf16[512,1152]{1,0:T(8,128)(2,1)}, u32[]{:S(2)}) %copy-start) | copy-done | bytes 1179672
  3.1 0.0 copy-start.1
  3.1 1.2 %copy-done.1 = f32[4,128,512]{2,1,0:T(8,128)S(1)} copy-done((f32[4,128,512]{2,1,0:T(8,128)S(1)}, f32[4,128,512]{2,1,0:T(8,128)}, u32[]{:S(2)}) %copy-start.1) | copy-done | bytes 1048600
  4.4 0.0 copy-start.2
  4.4 0.9 %copy-done.2 = bf16[2,256,128]{2,1,0:T(8,128)(2,1)S(1)} copy-done((bf16[2,256,128]{2,1,0:T(8,128)(2,1)S(1)}, bf16[2,256,128]{2,1,0:T(8,128)(2,1)}, u32[]{:S(2)}) %copy-start.2) | copy-done | bytes 131096
  5.3 0.0 copy-start.3
  5.3 0.7 copy-done.3
  6.0 0.0 copy-start.4
  6.0 0.7 copy-done.4
  6.7 0.0 copy-start.5
  6.7 0.7 copy-done.5
  7.4 0.0 copy-start.6
  7.4 0.7 copy-done.6
  8.1 0.0 copy-start.7
  8.1 0.7 copy-done.7
  8.7 69.3 %shard_map.104 = (f32[4,128,512]{2,1,0:T(8,128)S(1)}, f32[4,128,512]{2,1,0:T(8,128)S(1)}) custom-call(f32[4,128,512]{2,1,0:T(8,128)S(1)} %copy-done.1, bf16[4,512,64]{2,1,0:T(8,128)(2,1)S(1)} %copy.11.args_1_, f32[2,512]{1,0:T(2,128)S(1)} %copy-done.4, f32[1,64]{1,0:T(1,128)S(1)} %bitcast.1, s32[4,128]{1,0:T(4,128)S(1)} %copy-done.5, ...), custom_call_target="tpu_custom_call" | custom-call | tf_op jit(solution)/shard_map/pallas_call | solution.py:454
  78.0 1.0 %copy.14 = f32[4,128,512]{2,1,0:T(8,128)} copy(f32[4,128,512]{2,1,0:T(8,128)S(1)} %get-tuple-element.4) | data formatting | bytes 2097152
  79.0 1.0 %copy.15 = f32[4,128,512]{2,1,0:T(8,128)} copy(f32[4,128,512]{2,1,0:T(8,128)S(1)} %get-tuple-element.5) | data formatting | bytes 2097152
Async XLA Ops:
  1.9 1.3 %copy-start = (bf16[512,1152]{1,0:T(8,128)(2,1)S(1)}, bf16[512,1152]{1,0:T(8,128)(2,1)}, u32[]{:S(2)}) copy-start(bf16[512,1152]{1,0:T(8,128)(2,1)} %constant.8.clone.args_8_) | copy-start | bytes 3538948
  3.1 1.2 %copy-start.1 = (f32[4,128,512]{2,1,0:T(8,128)S(1)}, f32[4,128,512]{2,1,0:T(8,128)}, u32[]{:S(2)}) copy-start(f32[4,128,512]{2,1,0:T(8,128)} %args_0_.4) | copy-start | bytes 3145732
  4.4 0.9 %copy-start.2 = (bf16[2,256,128]{2,1,0:T(8,128)(2,1)S(1)}, bf16[2,256,128]{2,1,0:T(8,128)(2,1)}, u32[]{:S(2)}) copy-start(bf16[2,256,128]{2,1,0:T(8,128)(2,1)} %constant.6.clone.args_6_) | copy-start | bytes 393220
  5.3 0.7 copy-start.3
  6.0 0.7 copy-start.4
  6.7 0.7 copy-start.5
  7.4 0.7 copy-start.6
  8.1 0.7 copy-start.7

commit v2 on v1

v2 whole, which is shorter than its diff:
```python
import math

import jax
import jax.numpy as jnp
import numpy as np
from jax import lax
from jax.experimental import pallas as pl
from jax.experimental.pallas import tpu as pltpu
from jax.sharding import PartitionSpec as P

MESH = pl.DeviceIdType.MESH
F32, BF16 = jnp.float32, jnp.bfloat16
ROWS, MODES, COLV, NLON, KEEP = 4, 64, 512, 4096, 512
LON, ZS, PTS = 32, 16, 128
K1 = 9
SPEC = K1 * MODES
GROUP = 16
OWNER_STEP = LON // ROWS

C1, C3, RT = math.cos(math.pi / 8), math.sin(math.pi / 8), math.sqrt(0.5)


def tables():
    kk = np.arange(32)
    signed = np.concatenate([kk, -1 - kk])
    j = np.arange(256)
    angle = 2.0 * np.pi * ((j[:, None] * signed[None, :]) % 256) / 256.0
    cos, sin = np.cos(angle), np.sin(angle)
    re_in = np.concatenate([cos[:, :32], sin[:, :32], cos[:, 32:], sin[:, 32:]], axis=1)
    im_in = np.concatenate([-sin[:, :32], cos[:, :32], -sin[:, 32:], cos[:, 32:]], axis=1)
    wave = np.stack([re_in.reshape(2, PTS, 128), im_in.reshape(2, PTS, 128)], axis=1)
    wave = wave.reshape(2, 2 * PTS, 128)
    k1 = np.arange(K1)
    phase = 2.0 * np.pi * ((k1[:, None] * j[None, :]) % NLON) / NLON
    twist = np.stack([np.cos(phase), np.sin(phase)], axis=1)
    twist = twist.reshape(2 * K1, 2, PTS).transpose(1, 0, 2)
    pick = np.zeros((KEEP, K1, 128))
    for one in range(K1):
        for lane in range(128):
            part, at = lane // 32, lane % 32
            if part < 2:
                k = one + 16 * at
            elif 1 <= one <= 7:
                k = 16 * at + 16 - one
            else:
                continue
            pick[k, one, lane] = (1.0 if k == 0 else 2.0) / NLON
    pick = pick.transpose(1, 0, 2)
    return (
        jnp.asarray(wave.astype(jnp.bfloat16)),
        jnp.asarray(twist.astype(np.float32)),
        jnp.asarray(pick.astype(jnp.bfloat16)),
    )


def cosines(p):
    e = [p[0] + p[8], p[1] + p[7], p[2] + p[6], p[3] + p[5], p[4]]
    o = [p[0] - p[8], p[1] - p[7], p[2] - p[6], p[3] - p[5]]
    f0, f1 = e[0] + e[4], e[1] + e[3]
    f02 = f0 + e[2]
    g0, g1 = e[0] - e[4], RT * (e[1] - e[3])
    o2 = RT * o[2]
    a, b = o[0] + o2, o[0] - o2
    u, v = C1 * o[1] + C3 * o[3], C3 * o[1] - C1 * o[3]
    return [f02 + f1, a + u, g0 + g1, b + v, f0 - e[2], b - v, g0 - g1, a - u, f02 - f1]


def sines(q):
    h = [None, q[1] + q[7], q[2] + q[6], q[3] + q[5], q[4]]
    d = [None, q[1] - q[7], q[2] - q[6], q[3] - q[5]]
    r = RT * (d[1] + d[3])
    h2 = RT * h[2]
    m, n = h2 + h[4], h2 - h[4]
    u, v = C3 * h[1] + C1 * h[3], C1 * h[1] - C3 * h[3]
    return [None, u + m, r + d[2], v + n, d[1] - d[3], v - n, r - d[2], u - m]


def column_of(row, size):
    at = lax.broadcasted_iota(jnp.int32, (size, size), 0)
    to = lax.broadcasted_iota(jnp.int32, (size, size), 1)
    spread = jnp.where(at == to, jnp.broadcast_to(row, (size, size)), 0.0)
    return jnp.sum(spread, axis=1, keepdims=True)


def by_lane(values):
    part = values[:, 0:128] + values[:, 128:256] + values[:, 256:384] + values[:, 384:512]
    return jnp.sum(part, axis=0, keepdims=True)


def kernel(
    lats,
    b_hbm, e_hbm, gain_hbm, kappa_hbm, flags_hbm, counts_hbm, wave_hbm, twist_hbm, pick_hbm,
    b, tbuf, ubuf, coefs,
    e, gain_ref, kappa_ref, flags_ref, counts_ref, wave, twist, pick,
    y0, halo_out, halo_in, halo_in2,
    aux_g, aux_w, got_g, got_w, to_owner, raw_in, rows_in, zbuf, bbuf, gains, y1,
    spec, spec_out, spec_in, s_out, f_out, s_in, f_in, part, ar1, mid, ar2,
    ld, aux_s, aux_r, halo_s, halo_r, own_s, own_r, spec_s, spec_r, ret_s, ret_r, ar_s, ar_r,
):
    lat, me = lax.axis_index("lat"), lax.axis_index("lon")
    owner = lax.rem(me, OWNER_STEP) == 0
    other = jnp.logical_not(owner)
    place, odd = lax.div(me, OWNER_STEP), lax.rem(lat, 2)

    def row_at(spot):
        return spot + odd * (ROWS - 1 - 2 * spot)

    my_row = row_at(place)
    down, up = lax.rem(lat + lats - 1, lats), lax.rem(lat + 1, lats)

    small = [
        pltpu.make_async_copy(source, target, ld.at[at])
        for at, (source, target) in enumerate(
            [
                (flags_hbm, flags_ref),
                (counts_hbm, counts_ref),
                (kappa_hbm, kappa_ref),
                (gain_hbm, gain_ref),
            ]
        )
    ]
    loads = [pltpu.make_async_copy(e_hbm, e, ld.at[4])]
    loads += [pltpu.make_async_copy(b_hbm.at[r], b.at[r], ld.at[5 + r]) for r in range(ROWS)]
    for load in small + loads:
        load.start()
    owner_loads = [
        pltpu.make_async_copy(wave_hbm, wave, ld.at[9]),
        pltpu.make_async_copy(twist_hbm, twist, ld.at[10]),
        pltpu.make_async_copy(pick_hbm, pick, ld.at[11]),
    ]

    barrier = pltpu.get_barrier_semaphore()

    def greet(device):
        pl.semaphore_signal(barrier, inc=1, device_id=device, device_id_type=MESH)

    @pl.when(owner)
    def _():
        def greet_lon(o, carry):
            greet((lat, lax.rem(me + o, LON)))
            return carry

        def greet_lat(o, carry):
            greet((lax.rem(lat + o, lats), me))
            return carry

        lax.fori_loop(1, LON, greet_lon, 0)
        lax.fori_loop(1, lats, greet_lat, 0)
        for load in owner_loads:
            load.start()

    @pl.when(other)
    def _():
        for spot in range(ROWS):
            greet((lat, spot * OWNER_STEP))
        greet((down, me))
        greet((up, me))

    for load in small:
        load.wait()
    flags = flags_ref[...]
    factor = (
        (flags == 0).astype(F32) + 0.5 * (flags == 1).astype(F32) + 0.25 * (flags == 2).astype(F32)
    )
    weight = factor * counts_ref[...].astype(F32) * 0.25
    w_col = [column_of(weight[r : r + 1, :], PTS) for r in range(ROWS)]
    kappa = column_of(kappa_ref[...], MODES)
    for mode in range(2):
        for quarter in range(4):
            at = mode * 4 + quarter
            aux_g[at : at + 1, :] = gain_ref[mode : mode + 1, quarter * 128 : quarter * 128 + 128]

    loads[0].wait()
    norm_part = jnp.zeros((1, PTS), F32)
    for r in range(ROWS):
        loads[1 + r].wait()
        weighted = (w_col[r] * b[r]).astype(BF16)
        modes = lax.dot_general(
            e[r], weighted, (((1,), (1,)), ((), ())), preferred_element_type=F32
        )
        y0[r] = modes
        halo_out[r] = modes.astype(BF16)
        norm_part = norm_part + by_lane(b[r] * b[r])
    for r in range(ROWS):
        aux_w[r] = jnp.concatenate([weight[r : r + 1, :], norm_part], axis=0)

    @pl.when(owner)
    def _():
        pl.semaphore_wait(barrier, LON - 1 + lats - 1)

    @pl.when(other)
    def _():
        pl.semaphore_wait(barrier, ROWS + 2)

    def halo(source, target, at):
        copies = [
            pltpu.make_async_remote_copy(
                source.at[pl.ds(2 * way, 2)], target.at[1 - way],
                halo_s.at[at + way], halo_r.at[at + way],
                device_id=(peer, me), device_id_type=MESH,
            )
            for way, peer in ((0, down), (1, up))
        ]
        for copy in copies:
            copy.start()
        return copies

    def diffuse(rows, halos):
        low, high = lat > 0, lat < lats - 1
        ext = [jnp.where(low, halos[0, i].astype(F32), 0.0) for i in range(2)]
        ext += rows
        ext += [jnp.where(high, halos[1, i].astype(F32), 0.0) for i in range(2)]
        once = [
            ext[i] + kappa * (ext[i + 1] - 2.0 * ext[i] + ext[i - 1]) for i in range(1, 7)
        ]
        once[0] = jnp.where(low, once[0], 0.0)
        once[5] = jnp.where(high, once[5], 0.0)
        return [
            once[i] + kappa * (once[i + 1] - 2.0 * once[i] + once[i - 1]) for i in range(1, 5)
        ]

    first_halo = halo(halo_out, halo_in, 0)

    def to_owners(sends):
        for spot in range(ROWS):
            at, row = spot * OWNER_STEP, row_at(spot)

            @pl.when(me != at)
            def _():
                for source, target, sent, got in sends(row):
                    pltpu.make_async_remote_copy(
                        source, target, sent, got, device_id=(lat, at), device_id_type=MESH
                    ).start()

            @pl.when(me == at)
            def _():
                for source, target, sent, got in sends(row):
                    target[...] = source[...]

    mine8 = pl.ds(pl.multiple_of(8 * me, 8), 8)
    to_owners(
        lambda row: (
            (halo_out.at[row], raw_in.at[me], own_s.at[0], own_r.at[0]),
            (aux_g, got_g.at[mine8], aux_s.at[0], aux_r.at[0]),
            (aux_w.at[row], got_w.at[me], aux_s.at[1], aux_r.at[1]),
        )
    )
    for copy in first_halo:
        copy.wait()
    diffused = diffuse([y0[r] for r in range(ROWS)], halo_in)
    for r in range(ROWS):
        to_owner[r] = diffused[r].astype(BF16)
    to_owners(lambda row: ((to_owner.at[row], rows_in.at[me], own_s.at[1], own_r.at[1]),))

    def settle(buffer, count, semaphore):
        view = buffer.at[pl.ds(0, count)]
        pltpu.make_async_copy(view, view, semaphore).wait()

    def forward(source):
        def one(g, carry):
            c, rows = lax.div(g, 4), pl.ds(pl.multiple_of(lax.rem(g, 4) * GROUP, GROUP), GROUP)
            x = [source[2 * z + c, rows, :].astype(F32) for z in range(ZS)]
            p = [x[0]] + [x[z] + x[16 - z] for z in range(1, 8)] + [x[8]]
            q = [None] + [x[z] - x[16 - z] for z in range(1, 8)]
            real, imag = cosines(p), sines(q)
            for k1 in range(K1):
                to = pl.ds(pl.multiple_of(k1 * MODES + lax.rem(g, 4) * GROUP, GROUP), GROUP)
                if k1 == 0:
                    re, im = real[0], jnp.zeros_like(real[0])
                else:
                    cos = twist[c, pl.ds(2 * k1, 1), :]
                    sin = twist[c, pl.ds(2 * k1 + 1, 1), :]
                    if k1 == 8:
                        re, im = real[8] * cos, real[8] * sin
                    else:
                        re = real[k1] * cos - imag[k1] * sin
                        im = real[k1] * sin + imag[k1] * cos
                zbuf[c, to, 0:PTS] = re.astype(BF16)
                zbuf[c, to, PTS : 2 * PTS] = im.astype(BF16)
            return carry

        lax.fori_loop(0, 8, one, 0)

    def coefficients(rows):
        coef = jnp.dot(zbuf[0, rows, :], wave[0], preferred_element_type=F32)
        return coef + jnp.dot(zbuf[1, rows, :], wave[1], preferred_element_type=F32)

    def back(coef, rows):
        scaled = (coef * gains[rows, :]).astype(BF16)
        for c in range(2):
            bbuf[c, rows, :] = lax.dot_general(
                scaled, wave[c], (((1,), (1,)), ((), ())), preferred_element_type=F32
            )

    chunks = [pl.ds(at * 192, 192) for at in range(3)]

    def inverse(target):
        def one(g, carry):
            c, rows = lax.div(g, 4), pl.ds(pl.multiple_of(lax.rem(g, 4) * GROUP, GROUP), GROUP)
            real, imag = [], [None]
            for k1 in range(K1):
                at = pl.ds(pl.multiple_of(k1 * MODES + lax.rem(g, 4) * GROUP, GROUP), GROUP)
                re = bbuf[c, at, 0:PTS]
                if k1 == 0:
                    real.append(re)
                    continue
                im = bbuf[c, at, PTS : 2 * PTS]
                cos = twist[c, pl.ds(2 * k1, 1), :]
                sin = twist[c, pl.ds(2 * k1 + 1, 1), :]
                real.append(re * cos + im * sin)
                if k1 < 8:
                    imag.append(im * cos - re * sin)
            even, odds = cosines(real), sines(imag)
            target[c, rows, :] = even[0].astype(BF16)
            target[16 + c, rows, :] = even[8].astype(BF16)
            for z in range(1, 8):
                target[2 * z + c, rows, :] = (even[z] + odds[z]).astype(BF16)
                target[2 * (16 - z) + c, rows, :] = (even[z] - odds[z]).astype(BF16)
            return carry

        lax.fori_loop(0, 8, one, 0)

    def give(source_at, target, semaphores):
        def send(o):
            peer = lax.rem(me + o, LON)
            pltpu.make_async_remote_copy(
                source_at(peer), target, semaphores[0], semaphores[1],
                device_id=(lat, peer), device_id_type=MESH,
            ).start()

        def pair(o, carry):
            send(16 - o)
            send(16 + o)
            return carry

        send(16)
        lax.fori_loop(1, 16, pair, 0)

    @pl.when(owner)
    def _():
        for load in owner_loads:
            load.wait()
        mine = e[my_row]
        gram = lax.dot_general(mine, mine, (((1,), (1,)), ((), ())), preferred_element_type=F32)
        gram_high = gram.astype(BF16)
        gram_low = (gram - gram_high.astype(F32)).astype(BF16)
        gram_both = jnp.concatenate(
            [gram_high.astype(F32), gram_low.astype(F32)], axis=1
        ).astype(BF16)

        settle(got_g.reshape(LON, 8, 128), LON - 1, aux_r.at[0])
        settle(got_w, LON - 1, aux_r.at[1])
        spread = jnp.concatenate([got_g[pl.ds(q, MODES, stride=4), :] for q in range(4)], axis=1)
        first = spread.astype(BF16)
        rest = spread - first.astype(F32)
        second = rest.astype(BF16)
        third = (rest - second.astype(F32)).astype(BF16)
        for k1 in range(K1):
            total = jnp.dot(first, pick[k1], preferred_element_type=F32)
            total = total + jnp.dot(second, pick[k1], preferred_element_type=F32)
            total = total + jnp.dot(third, pick[k1], preferred_element_type=F32)
            gains[pl.ds(k1 * MODES, MODES), :] = total
        norm_sum = got_w[0, 1:2, :]
        for source in range(1, LON):
            norm_sum = norm_sum + got_w[source, 1:2, :]

        settle(rows_in, LON - 1, own_r.at[1])
        forward(rows_in)
        for rows in chunks:
            back(coefficients(rows), rows)
        inverse(s_out)

        for z in range(ZS):
            pair = jnp.concatenate([s_out[2 * z], s_out[2 * z + 1]], axis=1)
            product = jnp.dot(
                gram_both, jnp.concatenate([pair, pair], axis=0), preferred_element_type=F32
            )
            for c in range(2):
                row = got_w[2 * z + c, 0:1, :]
                y1[2 * z + c] = product[:, c * PTS : c * PTS + PTS] * (row * row)
        forward(y1)
        for rows in chunks:
            coef = coefficients(rows)
            spec[rows, :] = coef
            spec_out[rows, :] = coef.astype(BF16)

        lowest, highest = lax.div(ROWS - 1 - my_row, ROWS - 1), lax.div(my_row, ROWS - 1)
        turn = 1 - 2 * odd
        before = (
            lax.rem(lat - lowest + lats, lats), OWNER_STEP * (place - turn * (1 - lowest))
        )
        after = (
            lax.rem(lat + highest, lats), OWNER_STEP * (place + turn * (1 - highest))
        )
        exchange = [
            pltpu.make_async_remote_copy(
                spec_out, spec_in.at[slot], spec_s.at[slot], spec_r.at[slot],
                device_id=device, device_id_type=MESH,
            )
            for slot, device in ((1, before), (0, after))
        ]
        for copy in exchange:
            copy.start()

        for rows in chunks:
            back(spec[rows, :], rows)
        inverse(f_out)
        give(lambda peer: f_out.at[peer], f_in.at[my_row], (ret_s.at[1], ret_r.at[1]))
        give(lambda peer: s_out.at[peer], s_in.at[my_row], (ret_s.at[0], ret_r.at[0]))
        f_in[my_row] = f_out[me]
        s_in[my_row] = s_out[me]

        settle(raw_in, LON - 1, own_r.at[0])

        def products(source, carry):
            s = s_out[source].astype(F32)
            return (
                carry[0] + s * raw_in[source].astype(F32),
                carry[1] + s * y1[source],
            )

        empty = jnp.zeros((MODES, PTS), F32)
        bt, tt = lax.fori_loop(0, LON, products, (empty, empty))

        for copy in exchange:
            copy.wait()
        inner = lat * ROWS + my_row
        has_before, has_after = inner > 0, inner < lats * ROWS - 1
        tu = empty
        for k1 in range(K1):
            rows = pl.ds(k1 * MODES, MODES)
            here = spec[rows, :]
            prev = jnp.where(has_before, spec_in[0, rows, :].astype(F32), 0.0)
            post = jnp.where(has_after, spec_in[1, rows, :].astype(F32), 0.0)
            once = here + kappa * (post - 2.0 * here + prev)
            tu = tu + gains[rows, :] * once * once
        norm_sum = jnp.where(place == 0, norm_sum, 0.0)
        sums = [norm_sum] + [jnp.sum(v, axis=0, keepdims=True) for v in (bt, tt, tu)]
        lane = lax.broadcasted_iota(jnp.int32, (1, PTS), 1)
        packed = jnp.zeros((1, PTS), F32)
        for at, v in enumerate(sums):
            packed = jnp.where(lane == at, jnp.sum(v, axis=1, keepdims=True), packed)
        part[...] = packed

        def send_lat(o, carry):
            pltpu.make_async_remote_copy(
                part, ar1.at[lat], ar_s.at[0], ar_r.at[0],
                device_id=(lax.rem(lat + o, lats), me), device_id_type=MESH,
            ).start()
            return carry

        lax.fori_loop(1, lats, send_lat, 0)
        ar1[lat] = packed
        settle(ar1, lats - 1, ar_r.at[0])
        total = ar1[0]
        for at in range(1, lats):
            total = total + ar1[at]
        mid[...] = total
        give(lambda peer: mid, ar2.at[place], (ar_s.at[1], ar_r.at[1]))
        ar2[place] = total

    def expand(values, r):
        return w_col[r] * jnp.dot(values.T.astype(BF16), e[r], preferred_element_type=F32)

    def arrived(buffer, semaphore):
        @pl.when(owner)
        def _():
            settle(buffer, ROWS - 1, semaphore)

        @pl.when(other)
        def _():
            settle(buffer, ROWS, semaphore)

    arrived(f_in, ret_r.at[1])
    second_halo = halo(f_in, halo_in2, 2)
    arrived(s_in, ret_r.at[0])
    for r in range(ROWS):
        tbuf[r] = expand(s_in[r].astype(F32), r)
    for copy in second_halo:
        copy.wait()
    diffused = diffuse([f_in[r].astype(F32) for r in range(ROWS)], halo_in2)
    for r in range(ROWS):
        ubuf[r] = expand(diffused[r], r)

    arrived(ar2, ar_r.at[1])
    total = ar2[0] + ar2[1] + ar2[2] + ar2[3]
    norm = total[:, 0:1]
    m1, m2, m3 = total[:, 1:2] / norm, total[:, 2:3] / norm, total[:, 3:4] / norm
    alpha = 1.0 / (1.0 + m1)
    spread2 = m2 - m1 * m1
    spread3 = m3 - 3.0 * m1 * m2 + 2.0 * m1 * m1 * m1
    beta = alpha * alpha * spread2
    alpha_next = alpha * spread2 / (spread2 * (1.0 - beta) + alpha * spread3)
    along = alpha * m1 + beta
    x_b, x_t = alpha + alpha_next * along, -alpha_next * alpha
    r_b = alpha * m1 - alpha_next * along
    r_t = -(alpha + alpha_next * (along - alpha))
    r_u = alpha_next * alpha
    rows = [x_b, x_t, r_b, r_t, r_u]
    coefs[...] = jnp.concatenate(
        [jnp.broadcast_to(row, (1, PTS)) for row in rows] + [jnp.zeros((3, PTS), F32)], axis=0
    )

    def sent(rows):
        settle(aux_w, rows, aux_s.at[1])
        settle(got_g.reshape(LON, 8, 128), rows, aux_s.at[0])
        settle(to_owner, rows, own_s.at[0])
        settle(to_owner, rows, own_s.at[1])

    @pl.when(owner)
    def _():
        sent(ROWS - 1)
        settle(s_out, LON - 1, ret_s.at[0])
        settle(f_out, LON - 1, ret_s.at[1])
        settle(ar1, lats - 1, ar_s.at[0])
        settle(ar1, LON - 1, ar_s.at[1])

    @pl.when(other)
    def _():
        sent(ROWS)


def combine(b, t, u, coefs, x_hbm, r_hbm, x, r, sem):
    x_b, x_t, r_b, r_t, r_u = [coefs[at : at + 1, 0:1] for at in range(5)]
    writes = []
    for row in range(ROWS):
        x[row] = x_b * b[row] + x_t * t[row]
        r[row] = r_b * b[row] + r_t * t[row] + r_u * u[row]
        for at, (source, target) in enumerate(((x, x_hbm), (r, r_hbm))):
            write = pltpu.make_async_copy(source.at[row], target.at[row], sem.at[at, row])
            write.start()
            writes.append(write)
    for write in writes:
        write.wait()


def local(right_side, eofs, spectral_gain, diffusivity, flags, counts):
    lats = lax.axis_size("lat")
    wave, twist, pick = tables()
    hbm = pl.BlockSpec(memory_space=pltpu.HBM)
    vmem = pl.BlockSpec(memory_space=pltpu.VMEM)
    like = jax.ShapeDtypeStruct(right_side.shape, F32)
    dma, vm = pltpu.SemaphoreType.DMA, pltpu.VMEM

    def whole(*args):
        kernel(lats, *args)

    fields = pl.pallas_call(
        whole,
        out_shape=(like, like, like, jax.ShapeDtypeStruct((8, PTS), F32)),
        in_specs=[hbm] * 9,
        out_specs=(vmem,) * 4,
        scratch_shapes=[
            vm((ROWS, MODES, COLV), BF16),
            vm((2, KEEP), F32),
            vm((1, MODES), F32),
            vm((ROWS, PTS), jnp.int32),
            vm((ROWS, PTS), jnp.int32),
            vm((2, 2 * PTS, 128), BF16),
            vm((2, 2 * K1, PTS), F32),
            vm((K1, KEEP, 128), BF16),
            vm((ROWS, MODES, PTS), F32),
            vm((ROWS, MODES, PTS), BF16),
            vm((2, 2, MODES, PTS), BF16),
            vm((2, 2, MODES, PTS), BF16),
            vm((8, 128), F32),
            vm((ROWS, 2, PTS), F32),
            vm((LON * 8, 128), F32),
            vm((LON, 2, PTS), F32),
            vm((ROWS, MODES, PTS), BF16),
            vm((LON, MODES, PTS), BF16),
            vm((LON, MODES, PTS), BF16),
            vm((2, SPEC, 2 * PTS), BF16),
            vm((2, SPEC, 2 * PTS), F32),
            vm((SPEC, 128), F32),
            vm((LON, MODES, PTS), F32),
            vm((SPEC, 128), F32),
            vm((SPEC, 128), BF16),
            vm((2, SPEC, 128), BF16),
            vm((LON, MODES, PTS), BF16),
            vm((LON, MODES, PTS), BF16),
            vm((ROWS, MODES, PTS), BF16),
            vm((ROWS, MODES, PTS), BF16),
            vm((1, PTS), F32),
            vm((max(lats, LON), 1, PTS), F32),
            vm((1, PTS), F32),
            vm((ROWS, 1, PTS), F32),
            dma((12,)),
            dma((2,)),
            dma((2,)),
            dma((4,)),
            dma((4,)),
            dma((2,)),
            dma((2,)),
            dma((2,)),
            dma((2,)),
            dma((2,)),
            dma((2,)),
            dma((2,)),
            dma((2,)),
        ],
        compiler_params=pltpu.CompilerParams(
            collective_id=0, has_side_effects=True, vmem_limit_bytes=40 * 2**20
        ),
    )(*[
        pltpu.with_memory_space_constraint(each, pltpu.HBM)
        for each in (
            right_side, jnp.swapaxes(eofs, 1, 2), spectral_gain, diffusivity.reshape(1, MODES),
            flags, counts, wave, twist, pick,
        )
    ])
    return pl.pallas_call(
        combine,
        out_shape=(like, like),
        in_specs=[vmem] * 4,
        out_specs=(hbm, hbm),
        scratch_shapes=[
            vm((ROWS, PTS, COLV), F32),
            vm((ROWS, PTS, COLV), F32),
            dma((2, ROWS)),
        ],
        compiler_params=pltpu.CompilerParams(vmem_limit_bytes=16 * 2**20),
    )(*fields)


def solution(mesh):
    in_specs = (
        P("lat", "lon", None),
        P("lat", None, None),
        P("lon", None),
        P(),
        P("lat", "lon"),
        P("lat", "lon"),
    )
    out_specs = (P("lat", "lon", None), P("lat", "lon", None))
    return jax.shard_map(local, mesh=mesh, in_specs=in_specs, out_specs=out_specs, check_vma=False)
```

time: 80.4 us -> 62 us (0.77)
  local copies, waits for them, and re-layouts: 10 us -> 0 us
  Pallas kernels: 69.3 us -> 61.2 us
    unnamed x19 -> x0, local copies, waits for them, and re-layouts: 10 us -> none
    pallas_call x1 -> x2, Pallas kernels: 69.3 us -> 61.2 us  [the longest x1 59.7 us: local(): pl.pallas_call(whole, out_shape=(like, like, like, jax.ShapeDtypeStruct((...]
where the time goes in v2:
time: 62 us; the launch traced here: 61.9 us
  Pallas kernels  61.2 us (99%)
  between operations  0.64 us (1%)
    pallas_call x1, Pallas kernels, local(): pl.pallas_call(whole, out_shape=(like, like, like, jax.ShapeDtypeStruct((...  59.7 us
    pallas_call x1, Pallas kernels, local(): pl.pallas_call(combine, out_shape=(like, like), in_specs=[vmem] * 4, out_...  1.47 us

profile of v2, /device:TPU:1, one launch (start us, length us, event | category | flops | bytes accessed | tf_op | source)
XLA Modules:
  0.0 61.9 jit_solution(15210107272808678201)
XLA Ops:
  0.6 59.7 %shard_map.104 = (f32[4,128,512]{2,1,0:T(8,128)S(1)}, f32[4,128,512]{2,1,0:T(8,128)S(1)}, f32[4,128,512]{2,1,0:T(8,128)S(1)}, f32[8,128]{1,0:T(8,128)S(1)}) custom-call(f32[4,128,512]{2,1,0:T(8,128)} %args_0_.4, bf16[4,64,512]{2,1,0:T(8,128)(2,1)} %bitcast.2, f32[2,512]{1,0:T(2,128)} %args_2_.4, f32[1,64]{1,0:T(1,128)} %bitcast.3, s32[4,128]{1,0:T(4,128)} %args_4_.4, ...), custom_call_target="tpu_custom_call" | custom-call | tf_op jit(solution)/shard_map/pallas_call | solution.py:548
  60.4 1.5 %shard_map.105 = (f32[4,128,512]{2,1,0:T(8,128)}, f32[4,128,512]{2,1,0:T(8,128)}) custom-call(f32[4,128,512]{2,1,0:T(8,128)S(1)} %get-tuple-element.6.b, f32[4,128,512]{2,1,0:T(8,128)S(1)} %get-tuple-element.7.t, f32[4,128,512]{2,1,0:T(8,128)S(1)} %get-tuple-element.8.u, f32[8,128]{1,0:T(8,128)S(1)} %get-tuple-element.9.coefs), custom_call_target="tpu_custom_call" | custom-call | tf_op jit(solution)/shard_map/pallas_call | solution.py:612

commit v3 on v2

--- a/solution.py
+++ b/solution.py
@@ -15,7 +15,8 @@
 K1 = 9
 SPEC = K1 * MODES
 GROUP = 16
-OWNER_STEP = LON // ROWS
+OWNER_FIRST, OWNER_STEP = 2, 8
+NEAR = 16
 
 C1, C3, RT = math.cos(math.pi / 8), math.sin(math.pi / 8), math.sqrt(0.5)
 
@@ -98,9 +99,10 @@
     ld, aux_s, aux_r, halo_s, halo_r, own_s, own_r, spec_s, spec_r, ret_s, ret_r, ar_s, ar_r,
 ):
     lat, me = lax.axis_index("lat"), lax.axis_index("lon")
-    owner = lax.rem(me, OWNER_STEP) == 0
+    spots = [OWNER_FIRST + OWNER_STEP * spot for spot in range(ROWS)]
+    owner = (me - spots[0]) * (me - spots[1]) * (me - spots[2]) * (me - spots[3]) == 0
     other = jnp.logical_not(owner)
-    place, odd = lax.div(me, OWNER_STEP), lax.rem(lat, 2)
+    place, odd = lax.div(me - OWNER_FIRST, OWNER_STEP), lax.rem(lat, 2)
 
     def row_at(spot):
         return spot + odd * (ROWS - 1 - 2 * spot)
@@ -121,8 +123,6 @@
     ]
     loads = [pltpu.make_async_copy(e_hbm, e, ld.at[4])]
     loads += [pltpu.make_async_copy(b_hbm.at[r], b.at[r], ld.at[5 + r]) for r in range(ROWS)]
-    for load in small + loads:
-        load.start()
     owner_loads = [
         pltpu.make_async_copy(wave_hbm, wave, ld.at[9]),
         pltpu.make_async_copy(twist_hbm, twist, ld.at[10]),
@@ -144,15 +144,22 @@
             greet((lax.rem(lat + o, lats), me))
             return carry
 
-        lax.fori_loop(1, LON, greet_lon, 0)
+        lax.fori_loop(LON // 2, LON, greet_lon, 0)
+        lax.fori_loop(1, LON // 2, greet_lon, 0)
         lax.fori_loop(1, lats, greet_lat, 0)
+
+    for load in small + loads:
+        load.start()
+
+    @pl.when(owner)
+    def _():
         for load in owner_loads:
             load.start()
 
     @pl.when(other)
     def _():
         for spot in range(ROWS):
-            greet((lat, spot * OWNER_STEP))
+            greet((lat, spots[spot]))
         greet((down, me))
         greet((up, me))
 
@@ -223,7 +230,7 @@
 
     def to_owners(sends):
         for spot in range(ROWS):
-            at, row = spot * OWNER_STEP, row_at(spot)
+            at, row = spots[spot], row_at(spot)
 
             @pl.when(me != at)
             def _():
@@ -240,13 +247,13 @@
     mine8 = pl.ds(pl.multiple_of(8 * me, 8), 8)
     to_owners(
         lambda row: (
-            (halo_out.at[row], raw_in.at[me], own_s.at[0], own_r.at[0]),
             (aux_g, got_g.at[mine8], aux_s.at[0], aux_r.at[0]),
             (aux_w.at[row], got_w.at[me], aux_s.at[1], aux_r.at[1]),
+            (halo_out.at[row], raw_in.at[me], own_s.at[0], own_r.at[0]),
         )
     )
     for copy in first_halo:
-        copy.wait()
+        copy.wait_recv()
     diffused = diffuse([y0[r] for r in range(ROWS)], halo_in)
     for r in range(ROWS):
         to_owner[r] = diffused[r].astype(BF16)
@@ -279,7 +286,7 @@
                 zbuf[c, to, PTS : 2 * PTS] = im.astype(BF16)
             return carry
 
-        lax.fori_loop(0, 8, one, 0)
+        lax.fori_loop(0, 8, one, 0, unroll=4)
 
     def coefficients(rows):
         coef = jnp.dot(zbuf[0, rows, :], wave[0], preferred_element_type=F32)
@@ -318,23 +325,27 @@
                 target[2 * (16 - z) + c, rows, :] = (even[z] - odds[z]).astype(BF16)
             return carry
 
-        lax.fori_loop(0, 8, one, 0)
-
-    def give(source_at, target, semaphores):
-        def send(o):
-            peer = lax.rem(me + o, LON)
+        lax.fori_loop(0, 8, one, 0, unroll=4)
+
+    def give(source_at, target, semaphores, half):
+        def send(peer, carry):
             pltpu.make_async_remote_copy(
                 source_at(peer), target, semaphores[0], semaphores[1],
                 device_id=(lat, peer), device_id_type=MESH,
             ).start()
-
-        def pair(o, carry):
-            send(16 - o)
-            send(16 + o)
             return carry
 
-        send(16)
-        lax.fori_loop(1, 16, pair, 0)
+        mine = lax.div(me, NEAR) if half else 1 - lax.div(me, NEAR)
+        start, end = half * NEAR, half * NEAR + NEAR
+        middle = mine * me + (1 - mine) * end
+        lax.fori_loop(start, middle, send, 0)
+        lax.fori_loop(middle + mine, end, send, 0)
+
+    def give_f(half):
+        give(lambda peer: f_out.at[peer], f_in.at[my_row], (ret_s.at[1], ret_r.at[1]), half)
+
+    def give_s(half):
+        give(lambda peer: s_out.at[peer], s_in.at[my_row], (ret_s.at[0], ret_r.at[0]), half)
 
     @pl.when(owner)
     def _():
@@ -387,10 +398,10 @@
         lowest, highest = lax.div(ROWS - 1 - my_row, ROWS - 1), lax.div(my_row, ROWS - 1)
         turn = 1 - 2 * odd
         before = (
-            lax.rem(lat - lowest + lats, lats), OWNER_STEP * (place - turn * (1 - lowest))
+            lax.rem(lat - lowest + lats, lats), spots[0] + OWNER_STEP * (place - turn * (1 - lowest))
         )
         after = (
-            lax.rem(lat + highest, lats), OWNER_STEP * (place + turn * (1 - highest))
+            lax.rem(lat + highest, lats), spots[0] + OWNER_STEP * (place + turn * (1 - highest))
         )
         exchange = [
             pltpu.make_async_remote_copy(
@@ -405,8 +416,8 @@
         for rows in chunks:
             back(spec[rows, :], rows)
         inverse(f_out)
-        give(lambda peer: f_out.at[peer], f_in.at[my_row], (ret_s.at[1], ret_r.at[1]))
-        give(lambda peer: s_out.at[peer], s_in.at[my_row], (ret_s.at[0], ret_r.at[0]))
+        give_f(0)
+        give_f(1)
         f_in[my_row] = f_out[me]
         s_in[my_row] = s_out[me]
 
@@ -423,7 +434,7 @@
         bt, tt = lax.fori_loop(0, LON, products, (empty, empty))
 
         for copy in exchange:
-            copy.wait()
+            copy.wait_recv()
         inner = lat * ROWS + my_row
         has_before, has_after = inner > 0, inner < lats * ROWS - 1
         tu = empty
@@ -436,28 +447,47 @@
             tu = tu + gains[rows, :] * once * once
         norm_sum = jnp.where(place == 0, norm_sum, 0.0)
         sums = [norm_sum] + [jnp.sum(v, axis=0, keepdims=True) for v in (bt, tt, tu)]
-        lane = lax.broadcasted_iota(jnp.int32, (1, PTS), 1)
-        packed = jnp.zeros((1, PTS), F32)
-        for at, v in enumerate(sums):
-            packed = jnp.where(lane == at, jnp.sum(v, axis=1, keepdims=True), packed)
+        sums = [jnp.sum(v, axis=1, keepdims=True) for v in sums]
+        packed = jnp.concatenate([jnp.broadcast_to(v, (1, PTS)) for v in sums], axis=0)
         part[...] = packed
 
-        def send_lat(o, carry):
+        def send_lat(peer):
             pltpu.make_async_remote_copy(
                 part, ar1.at[lat], ar_s.at[0], ar_r.at[0],
-                device_id=(lax.rem(lat + o, lats), me), device_id_type=MESH,
+                device_id=(peer, me), device_id_type=MESH,
             ).start()
+
+        def by_offset(o, carry):
+            send_lat(lax.rem(lat + o, lats))
             return carry
 
-        lax.fori_loop(1, lats, send_lat, 0)
+        def by_distance(i, carry):
+            j = lax.div(i, 4)
+            side = lax.rem(j, 2)
+            dy = 4 + (1 - side) * lax.div(j, 2) - side * lax.div(j + 1, 2)
+            dx = lax.rem(2 + lax.rem(i, 4), 4)
+            x, y = lax.div(lat, 8), lax.rem(lat, 8)
+            send_lat(8 * lax.rem(x + dx, 4) + lax.rem(y + dy, 8))
+            return carry
+
+        if lats == 32:
+            lax.fori_loop(0, 30, by_distance, 0)
+            lax.fori_loop(31, 32, by_distance, 0)
+        else:
+            lax.fori_loop(1, lats, by_offset, 0)
+        give_s(0)
+        give_s(1)
         ar1[lat] = packed
         settle(ar1, lats - 1, ar_r.at[0])
         total = ar1[0]
         for at in range(1, lats):
             total = total + ar1[at]
         mid[...] = total
-        give(lambda peer: mid, ar2.at[place], (ar_s.at[1], ar_r.at[1]))
+        give(lambda peer: mid, ar2.at[place], (ar_s.at[1], ar_r.at[1]), 0)
+        give(lambda peer: mid, ar2.at[place], (ar_s.at[1], ar_r.at[1]), 1)
         ar2[place] = total
+        for copy in exchange:
+            copy.wait_send()
 
     def expand(values, r):
         return w_col[r] * jnp.dot(values.T.astype(BF16), e[r], preferred_element_type=F32)
@@ -477,15 +507,15 @@
     for r in range(ROWS):
         tbuf[r] = expand(s_in[r].astype(F32), r)
     for copy in second_halo:
-        copy.wait()
+        copy.wait_recv()
     diffused = diffuse([f_in[r].astype(F32) for r in range(ROWS)], halo_in2)
     for r in range(ROWS):
         ubuf[r] = expand(diffused[r], r)
 
     arrived(ar2, ar_r.at[1])
     total = ar2[0] + ar2[1] + ar2[2] + ar2[3]
-    norm = total[:, 0:1]
-    m1, m2, m3 = total[:, 1:2] / norm, total[:, 2:3] / norm, total[:, 3:4] / norm
+    norm = total[0:1]
+    m1, m2, m3 = total[1:2] / norm, total[2:3] / norm, total[3:4] / norm
     alpha = 1.0 / (1.0 + m1)
     spread2 = m2 - m1 * m1
     spread3 = m3 - 3.0 * m1 * m2 + 2.0 * m1 * m1 * m1
@@ -497,9 +527,10 @@
     r_t = -(alpha + alpha_next * (along - alpha))
     r_u = alpha_next * alpha
     rows = [x_b, x_t, r_b, r_t, r_u]
-    coefs[...] = jnp.concatenate(
-        [jnp.broadcast_to(row, (1, PTS)) for row in rows] + [jnp.zeros((3, PTS), F32)], axis=0
-    )
+    for at, row in enumerate(rows):
+        coefs[at : at + 1, :] = jnp.concatenate([row] * (COLV // PTS), axis=1)
+    for copy in first_halo + second_halo:
+        copy.wait_send()
 
     def sent(rows):
         settle(aux_w, rows, aux_s.at[1])
@@ -521,7 +552,7 @@
 
 
 def combine(b, t, u, coefs, x_hbm, r_hbm, x, r, sem):
-    x_b, x_t, r_b, r_t, r_u = [coefs[at : at + 1, 0:1] for at in range(5)]
+    x_b, x_t, r_b, r_t, r_u = [coefs[at : at + 1, :] for at in range(5)]
     writes = []
     for row in range(ROWS):
         x[row] = x_b * b[row] + x_t * t[row]
@@ -547,7 +578,7 @@
 
     fields = pl.pallas_call(
         whole,
-        out_shape=(like, like, like, jax.ShapeDtypeStruct((8, PTS), F32)),
+        out_shape=(like, like, like, jax.ShapeDtypeStruct((8, COLV), F32)),
         in_specs=[hbm] * 9,
         out_specs=(vmem,) * 4,
         scratch_shapes=[
@@ -581,10 +612,10 @@
             vm((LON, MODES, PTS), BF16),
             vm((ROWS, MODES, PTS), BF16),
             vm((ROWS, MODES, PTS), BF16),
-            vm((1, PTS), F32),
-            vm((max(lats, LON), 1, PTS), F32),
-            vm((1, PTS), F32),
-            vm((ROWS, 1, PTS), F32),
+            vm((4, PTS), F32),
+            vm((max(lats, LON), 4, PTS), F32),
+            vm((4, PTS), F32),
+            vm((ROWS, 4, PTS), F32),
             dma((12,)),
             dma((2,)),
             dma((2,)),

time: 62 us -> 60.8 us (0.981)
  Pallas kernels: 61.2 us -> 60 us
    pallas_call x1, Pallas kernels: 59.7 us -> 58.6 us  [local(): pl.pallas_call(whole, out_shape=(like, like, like, jax.ShapeDtypeStruct((...]
where the time goes in v3:
time: 60.8 us; the launch traced here: 60.6 us
  Pallas kernels  60 us (99%)
  between operations  0.64 us (1%)
    pallas_call x1, Pallas kernels, local(): pl.pallas_call(whole, out_shape=(like, like, like, jax.ShapeDtypeStruct((...  58.6 us
    pallas_call x1, Pallas kernels, local(): pl.pallas_call(combine, out_shape=(like, like), in_specs=[vmem] * 4, out_...  1.42 us

profile of v3, /device:TPU:1, one launch (start us, length us, event | category | flops | bytes accessed | tf_op | source)
XLA Modules:
  0.0 60.6 jit_solution(9312252084472602365)
XLA Ops:
  0.6 58.6 %shard_map.104 = (f32[4,128,512]{2,1,0:T(8,128)S(1)}, f32[4,128,512]{2,1,0:T(8,128)S(1)}, f32[4,128,512]{2,1,0:T(8,128)S(1)}, f32[8,512]{1,0:T(8,128)S(1)}) custom-call(f32[4,128,512]{2,1,0:T(8,128)} %args_0_.4, bf16[4,64,512]{2,1,0:T(8,128)(2,1)} %bitcast.2, f32[2,512]{1,0:T(2,128)} %args_2_.4, f32[1,64]{1,0:T(1,128)} %bitcast.3, s32[4,128]{1,0:T(4,128)} %args_4_.4, ...), custom_call_target="tpu_custom_call" | custom-call | tf_op jit(solution)/shard_map/pallas_call | solution.py:579
  59.2 1.4 %shard_map.105 = (f32[4,128,512]{2,1,0:T(8,128)}, f32[4,128,512]{2,1,0:T(8,128)}) custom-call(f32[4,128,512]{2,1,0:T(8,128)S(1)} %get-tuple-element.6.b, f32[4,128,512]{2,1,0:T(8,128)S(1)} %get-tuple-element.7.t, f32[4,128,512]{2,1,0:T(8,128)S(1)} %get-tuple-element.8.u, f32[8,512]{1,0:T(8,128)S(1)} %get-tuple-element.9.coefs), custom_call_target="tpu_custom_call" | custom-call | tf_op jit(solution)/shard_map/pallas_call | solution.py:643

commit v4 on v3

--- a/solution.py
+++ b/solution.py
@@ -15,7 +15,7 @@
 K1 = 9
 SPEC = K1 * MODES
 GROUP = 16
-OWNER_FIRST, OWNER_STEP = 2, 8
+OWNER_FIRST, OWNER_STEP = 3, 8
 NEAR = 16
 
 C1, C3, RT = math.cos(math.pi / 8), math.sin(math.pi / 8), math.sqrt(0.5)
@@ -390,11 +390,6 @@
                 row = got_w[2 * z + c, 0:1, :]
                 y1[2 * z + c] = product[:, c * PTS : c * PTS + PTS] * (row * row)
         forward(y1)
-        for rows in chunks:
-            coef = coefficients(rows)
-            spec[rows, :] = coef
-            spec_out[rows, :] = coef.astype(BF16)
-
         lowest, highest = lax.div(ROWS - 1 - my_row, ROWS - 1), lax.div(my_row, ROWS - 1)
         turn = 1 - 2 * odd
         before = (
@@ -403,15 +398,20 @@
         after = (
             lax.rem(lat + highest, lats), spots[0] + OWNER_STEP * (place + turn * (1 - highest))
         )
-        exchange = [
-            pltpu.make_async_remote_copy(
-                spec_out, spec_in.at[slot], spec_s.at[slot], spec_r.at[slot],
-                device_id=device, device_id_type=MESH,
-            )
-            for slot, device in ((1, before), (0, after))
-        ]
-        for copy in exchange:
-            copy.start()
+        for rows in chunks:
+            coef = coefficients(rows)
+            spec[rows, :] = coef
+            spec_out[rows, :] = coef.astype(BF16)
+            for slot, device in ((1, before), (0, after)):
+                pltpu.make_async_remote_copy(
+                    spec_out.at[rows], spec_in.at[slot, rows], spec_s.at[slot], spec_r.at[slot],
+                    device_id=device, device_id_type=MESH,
+                ).start()
+
+        def exchanged(semaphores):
+            for slot in range(2):
+                view = spec_in.at[slot]
+                pltpu.make_async_copy(view, view, semaphores.at[slot]).wait()
 
         for rows in chunks:
             back(spec[rows, :], rows)
@@ -433,8 +433,7 @@
         empty = jnp.zeros((MODES, PTS), F32)
         bt, tt = lax.fori_loop(0, LON, products, (empty, empty))
 
-        for copy in exchange:
-            copy.wait_recv()
+        exchanged(spec_r)
         inner = lat * ROWS + my_row
         has_before, has_after = inner > 0, inner < lats * ROWS - 1
         tu = empty
@@ -486,8 +485,7 @@
         give(lambda peer: mid, ar2.at[place], (ar_s.at[1], ar_r.at[1]), 0)
         give(lambda peer: mid, ar2.at[place], (ar_s.at[1], ar_r.at[1]), 1)
         ar2[place] = total
-        for copy in exchange:
-            copy.wait_send()
+        exchanged(spec_s)
 
     def expand(values, r):
         return w_col[r] * jnp.dot(values.T.astype(BF16), e[r], preferred_element_type=F32)

time: 60.8 us -> 57.8 us (0.951)
  Pallas kernels: 60 us -> 57 us
    pallas_call x1, Pallas kernels: 58.6 us -> 55.6 us  [local(): pl.pallas_call(whole, out_shape=(like, like, like, jax.ShapeDtypeStruct((...]
where the time goes in v4:
time: 57.8 us; the launch traced here: 57.7 us
  Pallas kernels  57 us (99%)
  between operations  0.64 us (1%)
    pallas_call x1, Pallas kernels, local(): pl.pallas_call(whole, out_shape=(like, like, like, jax.ShapeDtypeStruct((...  55.6 us
    pallas_call x1, Pallas kernels, local(): pl.pallas_call(combine, out_shape=(like, like), in_specs=[vmem] * 4, out_...  1.42 us

profile of v4, /device:TPU:1, one launch (start us, length us, event | category | flops | bytes accessed | tf_op | source)
XLA Modules:
  0.0 57.7 jit_solution(2225108477010389967)
XLA Ops:
  0.6 55.6 %shard_map.104 = (f32[4,128,512]{2,1,0:T(8,128)S(1)}, f32[4,128,512]{2,1,0:T(8,128)S(1)}, f32[4,128,512]{2,1,0:T(8,128)S(1)}, f32[8,512]{1,0:T(8,128)S(1)}) custom-call(f32[4,128,512]{2,1,0:T(8,128)} %args_0_.4, bf16[4,64,512]{2,1,0:T(8,128)(2,1)} %bitcast.2, f32[2,512]{1,0:T(2,128)} %args_2_.4, f32[1,64]{1,0:T(1,128)} %bitcast.3, s32[4,128]{1,0:T(4,128)} %args_4_.4, ...), custom_call_target="tpu_custom_call" | custom-call | tf_op jit(solution)/shard_map/pallas_call | solution.py:577
  56.2 1.4 %shard_map.105 = (f32[4,128,512]{2,1,0:T(8,128)}, f32[4,128,512]{2,1,0:T(8,128)}) custom-call(f32[4,128,512]{2,1,0:T(8,128)S(1)} %get-tuple-element.6.b, f32[4,128,512]{2,1,0:T(8,128)S(1)} %get-tuple-element.7.t, f32[4,128,512]{2,1,0:T(8,128)S(1)} %get-tuple-element.8.u, f32[8,512]{1,0:T(8,128)S(1)} %get-tuple-element.9.coefs), custom_call_target="tpu_custom_call" | custom-call | tf_op jit(solution)/shard_map/pallas_call | solution.py:641
